TPU v7x, 32 devices: a whole 2x2x4 slice. The times are simulated.
32 devices in a mesh: groups: 2 (over y), expert: 16 (over z, x, core), tensor: 1.
Axes of the slice: x: 2, y: 2, z: 4, core: 2. Of those that a mesh axis runs over, the one named last changes fastest.
Arguments:
- tokens: bfloat16 [4096, 3072], P(('groups', 'expert')), parts along dimension 0, may hold values from -6 to 6
- lengths: int32 [32], P(('groups', 'expert')), parts along dimension 0, may hold values from 32 to 128, as said below
- routed_expert: int32 [4096, 1], P(('groups', 'expert')), parts along dimension 0, may hold values from 0 to 1; in each aligned block of 128 rows (0 to 127, 128 to 255, ...) at most 80 rows name the same one
- attention_gain: float32 [3072], replicated, may hold values from 0.1 to 1.9
- w_query: bfloat16 [3072, 256], P('expert', 'tensor'), may hold values from -0.108253175 to 0.108253175
- w_key: bfloat16 [3072, 256], P('expert', 'tensor'), may hold values from -0.108253175 to 0.108253175
- w_value: bfloat16 [3072, 256], P('expert', 'tensor'), may hold values from -0.109375 to 0.109375
- w_out: bfloat16 [3072, 256], P('expert', 'tensor'), may hold values from -0.375 to 0.375
- expert_gain: float32 [3072], replicated, may hold values from 0.1 to 1.9
- w_gate: bfloat16 [3072, 16384], P(None, ('expert', 'tensor')), may hold values from -0.109375 to 0.109375
- w_up: bfloat16 [3072, 16384], P(None, ('expert', 'tensor')), may hold values from -0.109375 to 0.109375
- w_down: bfloat16 [16384, 3072], P(('expert', 'tensor')), may hold values from -0.0625 to 0.0625
Outputs:
- output: bfloat16 [4096, 3072], P(('groups', 'expert'), 'tensor'), parts along dimension 0
There are 2 independent parts, one for each index of `groups`. A program takes and returns all parts, laid end to end along the dimension named above; an argument that names none is the same for every part. Nothing has to cross between parts.
Inputs may be any that keep to these rules, and one draw needn't show every extreme that they name: `routed_expert`: in each aligned block of the 128 rows of one sequence, no expert is named by more than 80 rows, a bound that some block reaches. `lengths`: some sequence has all 128 positions valid, and some has the fewest that any sequence may have.
All inputs are finite; a program needn't handle non-finite values.
Results may differ from a plain program's by a relative error of at most 0.015.
Values may be sent and summed in bfloat16 or wider, within the bound.
A program may use at most 128 MiB of HBM per device.

v0:
```python
import jax
import jax.numpy as jnp
from jax import lax
from jax.sharding import PartitionSpec as P

HEAD = 128
GROUP = 8


def rms_scale(values, gain_vector):
    widened = values.astype(jnp.float32)
    mean_square = jnp.mean(widened * widened, axis=-1, keepdims=True)
    return (widened * lax.rsqrt(mean_square + 1e-05) * gain_vector).astype(jnp.bfloat16)


def slot_numbers(routed, experts, capacity):
    chosen = routed[:, 0]
    one_hot = (chosen[:, None] == jnp.arange(experts, dtype=jnp.int32)[None, :]).astype(jnp.int32)
    running = jnp.cumsum(one_hot, axis=0) - 1
    within = jnp.sum(running * one_hot, axis=1)
    return chosen * capacity + within


def attend(query_rows, key_rows, value_rows, length):
    token_count = query_rows.shape[0]
    head_shape = (token_count, query_rows.shape[1] // HEAD, HEAD)
    scores = jnp.einsum(
        "qhd,khd->hqk",
        query_rows.reshape(head_shape),
        key_rows.reshape(head_shape),
        preferred_element_type=jnp.float32,
    ) * HEAD ** (-0.5)
    positions = jnp.arange(token_count, dtype=jnp.int32)
    allowed = (positions[None, :] <= positions[:, None]) & (positions[None, :] < length)
    scores = jnp.where(allowed[None], scores, -1e30)
    weights = jax.nn.softmax(scores, axis=-1).astype(jnp.bfloat16)
    context = jnp.einsum(
        "hqk,khd->qhd", weights, value_rows.reshape(head_shape), preferred_element_type=jnp.float32
    ).astype(jnp.bfloat16)
    return context.reshape(token_count, -1)


def swiglu_part(arrived_block, gate_weight, up_weight, down_weight):
    gate_sum = jnp.einsum(
        "scd,df->scf", arrived_block, gate_weight, preferred_element_type=jnp.float32
    )
    upward = jnp.einsum("scd,df->scf", arrived_block, up_weight, preferred_element_type=jnp.float32)
    hidden = (jax.nn.silu(gate_sum) * upward).astype(jnp.bfloat16)
    return jnp.einsum("scf,fd->scd", hidden, down_weight, preferred_element_type=jnp.float32)


def body(
    tokens,
    lengths,
    routed_expert,
    attention_gain,
    w_query,
    w_key,
    w_value,
    w_out,
    expert_gain,
    w_gate,
    w_up,
    w_down,
):
    token_count = tokens.shape[0]
    model_width = tokens.shape[1]
    normed = rms_scale(tokens, attention_gain)
    query_sum = jnp.dot(
        normed,
        lax.all_gather(w_query, "expert", axis=0, tiled=True),
        preferred_element_type=jnp.float32,
    )
    key_sum = jnp.dot(
        normed,
        lax.all_gather(w_key, "expert", axis=0, tiled=True),
        preferred_element_type=jnp.float32,
    )
    value_sum = jnp.dot(
        normed,
        lax.all_gather(w_value, "expert", axis=0, tiled=True),
        preferred_element_type=jnp.float32,
    )
    context = attend(
        query_sum.astype(jnp.bfloat16),
        key_sum.astype(jnp.bfloat16),
        value_sum.astype(jnp.bfloat16),
        lengths[0],
    )
    partial_out = lax.dot_general(
        context,
        lax.all_gather(w_out, "expert", axis=0, tiled=True),
        (((1,), (1,)), ((), ())),
        preferred_element_type=jnp.float32,
    )
    cores = lax.axis_size("tensor")
    core_index = lax.axis_index("tensor")
    summed = lax.psum(partial_out, "tensor")
    after_attention = (tokens.astype(jnp.float32) + summed).astype(jnp.bfloat16)
    expert_input = rms_scale(after_attention, expert_gain)
    devices_along = lax.axis_size("expert")
    expert_count = devices_along // GROUP
    capacity = min(token_count, 2 * max(1, 5 * token_count // (8 * expert_count)))
    slot_ids = slot_numbers(routed_expert, expert_count, capacity)
    outgoing_all = (
        jnp.zeros((expert_count * capacity, model_width), jnp.bfloat16)
        .at[slot_ids]
        .set(expert_input)
    )
    outgoing_all = jnp.repeat(
        outgoing_all.reshape(expert_count, capacity, model_width), GROUP, axis=0
    )
    half_width = model_width // cores
    arrived = swiglu_part(
        lax.all_to_all(outgoing_all, "expert", split_axis=0, concat_axis=0, tiled=True),
        w_gate,
        w_up,
        w_down,
    )
    reduced = lax.psum_scatter(arrived, "tensor", scatter_dimension=2, tiled=True).astype(
        jnp.bfloat16
    )
    returned = lax.all_to_all(reduced, "expert", split_axis=0, concat_axis=0, tiled=True)
    part_sums = returned.reshape(expert_count, GROUP, capacity, half_width).astype(jnp.float32)
    expert_rows = jnp.sum(part_sums, axis=1).reshape(expert_count * capacity, half_width)[slot_ids]
    after_half = lax.dynamic_slice_in_dim(after_attention, core_index * half_width, half_width, 1)
    return (after_half.astype(jnp.float32) + expert_rows).astype(jnp.bfloat16)


def solution(mesh):
    return jax.shard_map(
        body,
        mesh=mesh,
        in_specs=(
            P(("groups", "expert"), None),
            P(("groups", "expert")),
            P(("groups", "expert"), None),
            P(),
            P("expert", "tensor"),
            P("expert", "tensor"),
            P("expert", "tensor"),
            P("expert", "tensor"),
            P(),
            P(None, ("expert", "tensor")),
            P(None, ("expert", "tensor")),
            P(("expert", "tensor"), None),
        ),
        out_specs=P(("groups", "expert"), "tensor"),
        check_vma=False,
    )
```

profile of v0, /device:TPU:11, one launch (start us, length us, event | category | flops | bytes accessed | tf_op | source)
XLA Modules:
  0.0 581.0 jit_solution(12763999732447808872)
XLA Ops:
  6.5 0.7 all-gather.5.cloned.1.call-update
  10.0 0.7 fusion.30
  10.9 0.8 select_reduce_fusion
  11.7 1.4 fusion.14
  13.1 0.7 fusion.33
  13.9 35.1 %all-gather.5.cloned.1.call-done = bf16[3072,256]{1,0:T(8,128)(2,1)} async-done(((bf16[192,256]{1,0:T(8,128)(2,1)}), bf16[3072,256]{1,0:T(8,128)(2,1)}) %all-gather.5.cloned.1.call-update) | async-done | bytes 1572880 | tf_op jit(solution)/shard_map/all_gather | solution.py:81
  49.0 2.1 convolution_convert_fusion.2
  51.2 38.7 %all-gather.7.cloned.1.call-done = bf16[3072,256]{1,0:T(8,128)(2,1)} async-done(((bf16[192,256]{1,0:T(8,128)(2,1)}), bf16[3072,256]{1,0:T(8,128)(2,1)}) %all-gather.7.cloned.1.call-update) | async-done | bytes 1572880 | tf_op jit(solution)/shard_map/all_gather | solution.py:71
  89.9 1.8 fusion.20
  91.8 39.0 %all-gather.9.cloned.1.call-done = bf16[3072,256]{1,0:T(8,128)(2,1)} async-done(((bf16[192,256]{1,0:T(8,128)(2,1)}), bf16[3072,256]{1,0:T(8,128)(2,1)}) %all-gather.9.cloned.1.call-update) | async-done | bytes 1572880 | tf_op jit(solution)/shard_map/all_gather | solution.py:76
  130.8 1.8 fusion.21
  133.1 38.5 %all-gather.11.cloned.1.call-done = bf16[3072,256]{1,0:T(8,128)(2,1)} async-done(((bf16[192,256]{1,0:T(8,128)(2,1)}), bf16[3072,256]{1,0:T(8,128)(2,1)}) %all-gather.11.cloned.1.call-update) | async-done | bytes 1572880 | tf_op jit(solution)/shard_map/all_gather | solution.py:92
  171.5 2.2 multiply_reduce_fusion
  173.7 2.1 scatter_custom_fusion
  175.8 1.0 broadcast_in_dim.19
  176.8 176.8 %all_to_all.10 = bf16[16,80,3072]{2,1,0:T(8,128)(2,1)S(1)} all-to-all(bf16[16,80,3072]{2,1,0:T(8,128)(2,1)S(1)} %bitcast.54), channel_id=1, replica_groups=mesh['groups'=2,'expert'=16,'tensor'=1] {'expert'}, dimensions={0} | all-to-all | bytes 15728640 | tf_op jit(solution)/shard_map/all_to_all | solution.py:115
  353.6 10.1 %fusion.3 = f32[16,80,1024]{2,1,0:T(8,128)} fusion(bf16[16,80,3072]{2,1,0:T(8,128)(2,1)S(1)} %all_to_all.10, bf16[3072,1024]{1,0:T(8,128)(2,1)S(1)} %bitcast.61), kind=kOutput, calls=%fused_computation.6 | convolution fusion | flops 8053063680 | bytes 19398656 | tf_op jit(solution)/shard_map/scd,df->scf/dot_general | solution.py:47
  363.8 12.2 %multiply_convert_fusion = bf16[16,80,1024]{2,1,0:T(8,128)(2,1)} fusion(f32[16,80,1024]{2,1,0:T(8,128)} %fusion.3, bf16[16,80,3072]{2,1,0:T(8,128)(2,1)S(1)} %all_to_all.10, bf16[3072,1024]{1,0:T(8,128)(2,1)S(1)} %bitcast.63), kind=kOutput, calls=%fused_computation.11 | convolution fusion | flops 8060928000 | bytes 22020096 | tf_op jit(solution)/shard_map/scd,df->scf/dot_general | solution.py:44
  376.0 12.1 %fusion.7 = bf16[16,80,3072]{2,1,0:T(8,128)(2,1)} fusion(bf16[16,80,1024]{2,1,0:T(8,128)(2,1)} %multiply_convert_fusion, bf16[1024,3072]{1,0:T(8,128)(2,1)S(1)} %bitcast.65), kind=kOutput, calls=%fused_computation.10 | convolution fusion | flops 8056995840 | bytes 16777216 | tf_op jit(solution)/shard_map/scf,fd->scd/dot_general | solution.py:49
  388.1 5.7 all-to-all-start.1
  393.8 171.1 %all-to-all-done.1 = bf16[16,80,3072]{2,1,0:T(8,128)(2,1)} async-done(((bf16[16,80,3072]{2,1,0:T(8,128)(2,1)}), bf16[16,80,3072]{2,1,0:T(8,128)(2,1)}, u32[]{:S(2)}, u32[]{:S(2)}) %all-to-all-start.1) | async-done | bytes 7864352 | tf_op jit(solution)/shard_map/all_to_all | solution.py:123
  564.9 4.8 convert_reduce_fusion
  569.7 2.3 gather_fusion
  572.0 2.5 add_convert_fusion
  (38 shorter events, 2.9 us)
Async XLA Ops:
  6.5 42.5 %all-gather.5.cloned.1.call-start = ((), (), s32[]{:S(2)}) async-start(), calls=%async_computation.2 | async-start | bytes 1671168 | tf_op jit(solution)/shard_map/all_gather | solution.py:81
  7.3 82.7 %all-gather.7.cloned.1.call-start = ((), (), s32[]{:S(2)}) async-start(), calls=%async_computation.3 | async-start | bytes 1671168 | tf_op jit(solution)/shard_map/all_gather | solution.py:71
  8.0 122.8 %all-gather.9.cloned.1.call-start = ((), (), s32[]{:S(2)}) async-start(), calls=%async_computation.4 | async-start | bytes 1671168 | tf_op jit(solution)/shard_map/all_gather | solution.py:76
  8.7 162.8 %all-gather.11.cloned.1.call-start = ((), (), s32[]{:S(2)}) async-start(), calls=%async_computation.5 | async-start | bytes 1671168 | tf_op jit(solution)/shard_map/all_gather | solution.py:92
  13.1 76.8 %copy-start = (bf16[128,3072]{1,0:T(8,128)(2,1)S(1)}, bf16[128,3072]{1,0:T(8,128)(2,1)}, u32[]{:S(2)}) copy-start(bf16[128,3072]{1,0:T(8,128)(2,1)} %param.12) | copy-start | bytes 2359300
  13.1 76.8 %copy-start.2 = (f32[3072]{0:T(1024)S(1)}, f32[3072]{0:T(1024)}, u32[]{:S(2)}) copy-start(f32[3072]{0:T(1024)} %param.15) | copy-start | bytes 36868
  171.5 2.2 copy-start.1
  175.8 177.8 %slice-start = ((s8[6291456]{0:T(1024)(128)(4,1)}), s8[4194304]{0:T(1024)(128)(4,1)S(1)}, s32[]{:S(2)}) async-start(s8[6291456]{0:T(1024)(128)(4,1)} %bitcast.60), calls=%async_computation.6 | async-start | bytes 8388608
  176.8 176.8 %slice-start.1 = ((s8[6291456]{0:T(1024)(128)(4,1)}), s8[2097152]{0:T(1024)(128)(4,1)S(1)}, s32[]{:S(2)}) async-start(s8[6291456]{0:T(1024)(128)(4,1)} %bitcast.60), calls=%async_computation.7 | async-start | bytes 4194304
  176.8 186.9 %slice-start.2 = ((s8[6291456]{0:T(1024)(128)(4,1)}), s8[2097152]{0:T(1024)(128)(4,1)S(1)}, s32[]{:S(2)}) async-start(s8[6291456]{0:T(1024)(128)(4,1)} %bitcast.62), calls=%async_computation.8 | async-start | bytes 4194304
  353.6 10.2 %slice-start.3 = ((s8[6291456]{0:T(1024)(128)(4,1)}), s8[4194304]{0:T(1024)(128)(4,1)S(1)}, s32[]{:S(2)}) async-start(s8[6291456]{0:T(1024)(128)(4,1)} %bitcast.62), calls=%async_computation.9 | async-start | bytes 8388608
  353.6 22.4 %slice-start.4 = ((s8[6291456]{0:T(1024)(128)(4,1)}), s8[2097152]{0:T(1024)(128)(4,1)S(1)}, s32[]{:S(2)}) async-start(s8[6291456]{0:T(1024)(128)(4,1)} %bitcast.64), calls=%async_computation.10 | async-start | bytes 4194304
  363.7 12.2 %slice-start.5 = ((s8[6291456]{0:T(1024)(128)(4,1)}), s8[4194304]{0:T(1024)(128)(4,1)S(1)}, s32[]{:S(2)}) async-start(s8[6291456]{0:T(1024)(128)(4,1)} %bitcast.64), calls=%async_computation.11 | async-start | bytes 8388608
  388.1 176.8 %all-to-all-start.1 = ((bf16[16,80,3072]{2,1,0:T(8,128)(2,1)}), bf16[16,80,3072]{2,1,0:T(8,128)(2,1)}, u32[]{:S(2)}, u32[]{:S(2)}) async-start(bf16[16,80,3072]{2,1,0:T(8,128)(2,1)} %fusion.7), calls=%async_computation.1 | async-start | bytes 15728640 | tf_op jit(solution)/shard_map/all_to_all | solution.py:123
Sparse Core Ops, SparseCore 0:
  9.6 39.3 all-gather.4
  51.3 38.5 all-gather.6
  92.2 38.5 all-gather.8
  132.9 38.5 all-gather.10
where the time goes:
time: 582 us; the launch traced here: 581 us
  waiting for transfers between devices  325 us (56%)
  blocking collectives  177 us (30%)
  matrix products  42.7 us (7%)
  between operations  13.9 us (2%)
  other arithmetic  13.4 us (2%)
    all_to_all x1, blocking collectives, body(): lax.all_to_all(outgoing_all, 'expert', split_axis=0, concat_axis=0, tiled...  177 us
    all_to_all x1, waiting for transfers between devices, body(): lax.all_to_all(reduced, 'expert', split_axis=0, concat_axis=0, tiled=True)  171 us
    all_gather x1, waiting for transfers between devices, body(): lax.all_gather(w_key, 'expert', axis=0, tiled=True)  39 us
    all_gather x1, waiting for transfers between devices, body(): lax.all_gather(w_query, 'expert', axis=0, tiled=True)  38.7 us
    all_gather x1, waiting for transfers between devices, body(): lax.all_gather(w_out, 'expert', axis=0, tiled=True)  38.5 us
    all_gather x1, waiting for transfers between devices, body(): lax.all_gather(w_value, 'expert', axis=0, tiled=True)  35.1 us
    dot_general x1, matrix products, swiglu_part(): jnp.einsum('scd,df->scf', arrived_block, gate_weight, preferred_element_t...  12.2 us
    dot_general x1, matrix products, swiglu_part(): jnp.einsum('scf,fd->scd', hidden, down_weight, preferred_element_type=jnp...  12.1 us
  transfers between devices with their start and end apart: 5, of which 5 were waited for; matrix products, arithmetic and copies ran while one was open for 2% of the time, Pallas kernels for 0%

commit v1 on v0

--- a/solution.py
+++ b/solution.py
@@ -1,6 +1,10 @@
+import functools
+
 import jax
 import jax.numpy as jnp
 from jax import lax
+from jax.experimental import pallas as pl
+from jax.experimental.pallas import tpu as pltpu
 from jax.sharding import PartitionSpec as P
 
 HEAD = 128
@@ -127,9 +131,499 @@
     return (after_half.astype(jnp.float32) + expert_rows).astype(jnp.bfloat16)
 
 
+BF16 = jnp.bfloat16
+F32 = jnp.float32
+VMEM_BYTES = 60 * 1024 * 1024
+TILES = 4
+
+
+def remote(src, dst, send, recv, target):
+    return pltpu.make_async_remote_copy(
+        src_ref=src,
+        dst_ref=dst,
+        send_sem=send,
+        recv_sem=recv,
+        device_id={"expert": target},
+        device_id_type=pl.DeviceIdType.MESH,
+    )
+
+
+def greet(targets):
+    barrier = pltpu.get_barrier_semaphore()
+    for target in targets:
+        pl.semaphore_signal(
+            barrier, inc=1, device_id={"expert": target}, device_id_type=pl.DeviceIdType.MESH
+        )
+    pl.semaphore_wait(barrier, len(targets))
+
+
+def place():
+    me = lax.axis_index("expert")
+    core = me % 2
+    x = (me // 2) % 2
+    z = me // 4
+    return me, core, x, z
+
+
+def gather_kernel(
+    lengths, tokens, w_qkv, w_out, gain, egain, after, ein, qkv_full, out_full, normed, ctx, send, recv, local
+):
+    me, core, x, z = place()
+    shard = w_out.shape[0]
+    sib = me + 1 - 2 * core
+    across = me + 2 - 4 * x
+    def rows(who):
+        return pl.ds(pl.multiple_of(who * shard, 64), shard)
+
+    fulls = (qkv_full, out_full)
+    copies = []
+    for g, own in enumerate((w_qkv, w_out)):
+        copy = pltpu.make_async_copy(own, fulls[g].at[rows(me)], local.at[g])
+        copy.start()
+        copies.append(copy)
+    wide = tokens[...].astype(F32)
+    mean_square = jnp.mean(wide * wide, axis=-1, keepdims=True)
+    normed[...] = (wide * lax.rsqrt(mean_square + 1e-05) * gain[...]).astype(BF16)
+    for copy in copies:
+        copy.wait()
+    greet((sib, across, (me + 4) % 16, (me + 12) % 16))
+
+    targets = (me + 4, me - 4, across, sib)
+
+    def move(g, direction, who):
+        block = fulls[g].at[rows(who)]
+        return remote(block, block, send.at[g, direction, who], recv.at[g, who], targets[direction])
+
+    def arrived(g, who):
+        block = fulls[g].at[rows(who)]
+        remote(block, block, send.at[g, 0, who], recv.at[g, who], sib).wait_recv()
+
+    def each_up(who, act, g):
+        @pl.when(z < 3)
+        def _():
+            act(move(g, 0, who))
+
+    def each_down(who, act, g):
+        @pl.when(z > 0)
+        def _():
+            act(move(g, 1, who))
+
+    def start(copy):
+        copy.start()
+
+    def finish(copy):
+        copy.wait_send()
+
+    def column(g, act, wait):
+        each_up(me, act, g)
+        each_down(me, act, g)
+        act(move(g, 2, me))
+        act(move(g, 3, me))
+        for d in (1, 2, 3):
+
+            @pl.when(z >= d)
+            def _():
+                who = me - 4 * d
+                if wait:
+                    arrived(g, who)
+                each_up(who, act, g)
+                act(move(g, 2, who))
+                act(move(g, 3, who))
+
+            @pl.when(z + d <= 3)
+            def _():
+                who = me + 4 * d
+                if wait:
+                    arrived(g, who)
+                each_down(who, act, g)
+                act(move(g, 2, who))
+                act(move(g, 3, who))
+
+        def pass_on(who):
+            if wait:
+                arrived(g, who)
+            act(move(g, 3, who))
+
+        pass_on(across)
+        for d in (1, 2, 3):
+
+            @pl.when(z >= d)
+            def _():
+                pass_on(across - 4 * d)
+
+            @pl.when(z + d <= 3)
+            def _():
+                pass_on(across + 4 * d)
+
+    def siblings(g):
+        for zz in range(4):
+            for xx in range(2):
+                arrived(g, (zz * 2 + xx) * 2 + 1 - core)
+
+    column(0, start, True)
+    column(1, start, True)
+    siblings(0)
+
+    width = qkv_full.shape[1] // 3
+    qkv = jnp.dot(normed[...], qkv_full[...], preferred_element_type=F32).astype(BF16)
+    count = tokens.shape[0]
+    qpos = lax.broadcasted_iota(jnp.int32, (count, count), 0)
+    kpos = lax.broadcasted_iota(jnp.int32, (count, count), 1)
+    allowed = (kpos <= qpos) & (kpos < lengths[...])
+    for head in range(width // HEAD):
+        at = head * HEAD
+        query = qkv[:, at : at + HEAD]
+        key = qkv[:, width + at : width + at + HEAD]
+        value = qkv[:, 2 * width + at : 2 * width + at + HEAD]
+        scores = lax.dot_general(
+            query, key, (((1,), (1,)), ((), ())), preferred_element_type=F32
+        ) * HEAD ** (-0.5)
+        scores = jnp.where(allowed, scores, -1e30)
+        peak = jnp.max(scores, axis=-1, keepdims=True)
+        weights = jnp.exp(scores - peak)
+        weights = (weights / jnp.sum(weights, axis=-1, keepdims=True)).astype(BF16)
+        ctx[:, at : at + HEAD] = jnp.dot(weights, value, preferred_element_type=F32).astype(BF16)
+    siblings(1)
+    attended = lax.dot_general(
+        ctx[...], out_full[...], (((1,), (1,)), ((), ())), preferred_element_type=F32
+    )
+    after[...] = (tokens[...].astype(F32) + attended).astype(BF16)
+    wide = after[...].astype(F32)
+    mean_square = jnp.mean(wide * wide, axis=-1, keepdims=True)
+    ein[...] = (wide * lax.rsqrt(mean_square + 1e-05) * egain[...]).astype(BF16)
+    column(0, finish, False)
+    column(1, finish, False)
+
+
+def expert_kernel(
+    half_a,
+    ein,
+    after,
+    perm,
+    perm_t,
+    w_gate,
+    w_up,
+    w_down,
+    out,
+    gate_v,
+    up_v,
+    down_v,
+    rows_in,
+    far_own,
+    hidden,
+    part,
+    from_sib,
+    diag_x,
+    diag_z,
+    sum_x,
+    sum_z,
+    near_sum,
+    far_sum,
+    far_back,
+    wsem,
+    gsend,
+    grecv,
+    csem,
+    rsend,
+    rrecv,
+    fsend,
+    frecv,
+):
+    me, core, x, z = place()
+    near = z // 2
+    sib = me + 1 - 2 * core
+    across = me + 2 - 4 * x
+    along = me + 4 - 8 * (z % 2)
+    mirror = me + 8 - 16 * near
+    slots, cap, width = rows_in.shape[1], rows_in.shape[2], rows_in.shape[3]
+    loads = []
+    for k, (src, dst) in enumerate(((w_gate, gate_v), (w_up, up_v), (w_down, down_v))):
+        copy = pltpu.make_async_copy(src, dst, wsem.at[k])
+        copy.start()
+        loads.append(copy)
+    far_own[...] = jnp.dot(perm[1 - near], ein[...], preferred_element_type=F32).astype(BF16)
+    rows_in[0, 0] = jnp.dot(perm[near], ein[...], preferred_element_type=F32).astype(BF16)
+    greet((sib, across, along, mirror))
+
+    started = []
+
+    def go(copy):
+        copy.start()
+        started.append(copy)
+        return copy
+
+    def gather_own(k):
+        own = rows_in.at[k, 0]
+        to_x = go(remote(own, rows_in.at[k, 1], gsend.at[k, 0], grecv.at[k, 0], across))
+        to_z = go(remote(own, rows_in.at[k, 2], gsend.at[k, 1], grecv.at[k, 1], along))
+        to_s = go(remote(own, rows_in.at[k, 4], gsend.at[k, 2], grecv.at[k, 2], sib))
+        return to_x, to_z, to_s
+
+    def gather_pass(k, first):
+        first[0].wait_recv()
+        from_x = rows_in.at[k, 1]
+        rest = cap - half_a
+        d_z = go(
+            remote(
+                from_x.at[pl.ds(half_a, rest)],
+                rows_in.at[k, 3, pl.ds(half_a, rest)],
+                gsend.at[k, 3],
+                grecv.at[k, 3],
+                along,
+            )
+        )
+        s1 = go(remote(from_x, rows_in.at[k, 5], gsend.at[k, 4], grecv.at[k, 4], sib))
+        first[1].wait_recv()
+        from_z = rows_in.at[k, 2]
+        d_x = go(
+            remote(
+                from_z.at[pl.ds(0, half_a)],
+                rows_in.at[k, 3, pl.ds(0, half_a)],
+                gsend.at[k, 5],
+                grecv.at[k, 5],
+                across,
+            )
+        )
+        s2 = go(remote(from_z, rows_in.at[k, 6], gsend.at[k, 6], grecv.at[k, 6], sib))
+        return d_z, d_x, s1, s2
+
+    def gather_last(k, second):
+        second[0].wait_recv()
+        second[1].wait_recv()
+        return go(
+            remote(rows_in.at[k, 3], rows_in.at[k, 7], gsend.at[k, 7], grecv.at[k, 7], sib)
+        )
+
+    def gather_done(first, second, third):
+        first[2].wait_recv()
+        second[2].wait_recv()
+        second[3].wait_recv()
+        third.wait_recv()
+
+    fan = gate_v.shape[1] // TILES
+    tile = width // TILES
+
+    def up_tile(k, t):
+        cols = pl.ds(pl.multiple_of(t * fan, fan), fan)
+        given = rows_in[k].reshape(slots * cap, width)
+        gate = jnp.dot(given, gate_v[:, cols], preferred_element_type=F32)
+        upward = jnp.dot(given, up_v[:, cols], preferred_element_type=F32)
+        hidden[:, cols] = (jax.nn.silu(gate) * upward).astype(BF16)
+
+    def down_tile(k, t):
+        cols = pl.ds(pl.multiple_of(t * tile, tile), tile)
+        total = jnp.dot(hidden[...], down_v[:, cols], preferred_element_type=F32)
+        part[k * TILES + t] = total.astype(BF16).reshape(slots, cap, tile)
+
+    def summing(kind, i):
+        rest = cap - half_a
+        ends = (
+            (part.at[i, pl.ds(4, 4)], from_sib.at[i], sib),
+            (part.at[i, 3, pl.ds(0, half_a)], diag_x.at[i], across),
+            (part.at[i, 3, pl.ds(half_a, rest)], diag_z.at[i], along),
+            (part.at[i, 1], sum_x.at[i], across),
+            (part.at[i, 2], sum_z.at[i], along),
+        )[kind]
+        return remote(ends[0], ends[1], rsend.at[kind, i], rrecv.at[kind, i], ends[2])
+
+    def plus(a, b):
+        return (a.astype(F32) + b.astype(F32)).astype(BF16)
+
+    def step_core(i):
+        summing(0, i).wait_recv()
+        part[i, 3] = plus(part[i, 3], from_sib[i, 3])
+        summing(1, i).start()
+        summing(2, i).start()
+        part[i, 0:3] = plus(part[i, 0:3], from_sib[i, 0:3])
+
+    def step_diag(i):
+        summing(1, i).wait_recv()
+        part[i, 2, 0:half_a] = plus(part[i, 2, 0:half_a], diag_x[i])
+        summing(4, i).start()
+        summing(2, i).wait_recv()
+        part[i, 1, half_a:cap] = plus(part[i, 1, half_a:cap], diag_z[i])
+        summing(3, i).start()
+
+    def total_of(i):
+        summing(3, i).wait_recv()
+        summing(4, i).wait_recv()
+        total = part[i, 0].astype(F32) + sum_x[i].astype(F32) + sum_z[i].astype(F32)
+        return total.astype(BF16)
+
+    def returning(t):
+        return remote(far_sum.at[t], far_back.at[t], fsend.at[t], frecv.at[t], mirror)
+
+    def loop(body):
+        lax.fori_loop(0, TILES, lambda t, c: (body(t), c)[1], 0)
+
+    near_first = gather_own(0)
+    crossing = go(remote(far_own, rows_in.at[1, 0], csem.at[0], csem.at[1], mirror))
+    near_second = gather_pass(0, near_first)
+    near_third = gather_last(0, near_second)
+    crossing.wait_recv()
+    far_first = gather_own(1)
+    gather_done(near_first, near_second, near_third)
+    for copy in loads:
+        copy.wait()
+    loop(functools.partial(up_tile, 0))
+    far_second = gather_pass(1, far_first)
+
+    def near_down(t):
+        down_tile(0, t)
+        summing(0, t).start()
+
+        @pl.when(t > 0)
+        def _():
+            step_core(t - 1)
+
+    loop(near_down)
+    step_core(TILES - 1)
+    far_third = gather_last(1, far_second)
+    gather_done(far_first, far_second, far_third)
+
+    def far_up(t):
+        up_tile(1, t)
+        step_diag(t)
+
+    loop(far_up)
+
+    def far_down(t):
+        i = TILES + t
+        down_tile(1, t)
+        summing(0, i).start()
+
+        @pl.when(t > 0)
+        def _():
+            step_core(i - 1)
+
+        near_sum[t] = total_of(t)
+
+    loop(far_down)
+    step_core(2 * TILES - 1)
+    loop(lambda t: step_diag(TILES + t))
+
+    def far_total(t):
+        far_sum[t] = total_of(TILES + t)
+        returning(t).start()
+
+    loop(far_total)
+
+    def finish(t):
+        cols = pl.ds(pl.multiple_of(t * tile, tile), tile)
+        returning(t).wait_recv()
+        moved = jnp.dot(perm_t[near], near_sum[t], preferred_element_type=F32)
+        moved = moved + jnp.dot(perm_t[1 - near], far_back[t], preferred_element_type=F32)
+        out[:, cols] = (after[:, cols].astype(F32) + moved).astype(BF16)
+        returning(t).wait_send()
+
+    loop(finish)
+    for copy in started:
+        copy.wait_send()
+
+    def drain(i, c):
+        for kind in range(5):
+            summing(kind, i).wait_send()
+        return c
+
+    lax.fori_loop(0, 2 * TILES, drain, 0)
+
+
+def fast_body(
+    tokens,
+    lengths,
+    routed_expert,
+    attention_gain,
+    w_query,
+    w_key,
+    w_value,
+    w_out,
+    expert_gain,
+    w_gate,
+    w_up,
+    w_down,
+):
+    count, width = tokens.shape
+    devices = lax.axis_size("expert")
+    experts = devices // GROUP
+    capacity = min(count, 2 * max(1, 5 * count // (8 * experts)))
+    vmem = pl.BlockSpec(memory_space=pltpu.VMEM)
+    anywhere = pl.BlockSpec(memory_space=pl.ANY)
+    heads = w_query.shape[1]
+    w_qkv = jnp.concatenate([w_query, w_key, w_value], axis=1)
+    dma = pltpu.SemaphoreType.DMA
+    after, ein = pl.pallas_call(
+        gather_kernel,
+        out_shape=[jax.ShapeDtypeStruct((count, width), BF16)] * 2,
+        in_specs=[vmem] * 6,
+        out_specs=[vmem] * 2,
+        scratch_shapes=[
+            pltpu.VMEM((width, 3 * heads), BF16),
+            pltpu.VMEM((width, heads), BF16),
+            pltpu.VMEM((count, width), BF16),
+            pltpu.VMEM((count, heads), BF16),
+            dma((2, 4, devices)),
+            dma((2, devices)),
+            dma((2,)),
+        ],
+        compiler_params=pltpu.CompilerParams(
+            collective_id=0, has_side_effects=True, vmem_limit_bytes=VMEM_BYTES
+        ),
+    )(
+        lengths.reshape(1, 1),
+        tokens,
+        w_qkv,
+        w_out,
+        attention_gain.reshape(1, width),
+        expert_gain.reshape(1, width),
+    )
+    slot_ids = slot_numbers(routed_expert, experts, capacity)
+    slots = jnp.arange(experts * capacity, dtype=jnp.int32)
+    perm = (slots[:, None] == slot_ids[None, :]).astype(BF16)
+    perm = perm.reshape(experts, capacity, count)
+    perm_t = jnp.swapaxes(perm, 1, 2)
+    units = w_gate.shape[1]
+    tile = width // TILES
+    half_a = capacity * 3 // 5 // 16 * 16
+    return pl.pallas_call(
+        functools.partial(expert_kernel, half_a),
+        out_shape=jax.ShapeDtypeStruct((count, width), BF16),
+        in_specs=[vmem] * 4 + [anywhere] * 3,
+        out_specs=vmem,
+        scratch_shapes=[
+            pltpu.VMEM((width, units), BF16),
+            pltpu.VMEM((width, units), BF16),
+            pltpu.VMEM((units, width), BF16),
+            pltpu.VMEM((2, 8, capacity, width), BF16),
+            pltpu.VMEM((capacity, width), BF16),
+            pltpu.VMEM((8 * capacity, units), BF16),
+            pltpu.VMEM((2 * TILES, 8, capacity, tile), BF16),
+            pltpu.VMEM((2 * TILES, 4, capacity, tile), BF16),
+            pltpu.VMEM((2 * TILES, half_a, tile), BF16),
+            pltpu.VMEM((2 * TILES, capacity - half_a, tile), BF16),
+            pltpu.VMEM((2 * TILES, capacity, tile), BF16),
+            pltpu.VMEM((2 * TILES, capacity, tile), BF16),
+            pltpu.VMEM((TILES, capacity, tile), BF16),
+            pltpu.VMEM((TILES, capacity, tile), BF16),
+            pltpu.VMEM((TILES, capacity, tile), BF16),
+            dma((3,)),
+            dma((2, 8)),
+            dma((2, 8)),
+            dma((2,)),
+            dma((5, 2 * TILES)),
+            dma((5, 2 * TILES)),
+            dma((TILES,)),
+            dma((TILES,)),
+        ],
+        compiler_params=pltpu.CompilerParams(
+            collective_id=1, has_side_effects=True, vmem_limit_bytes=VMEM_BYTES
+        ),
+    )(ein, after, perm, perm_t, w_gate, w_up, w_down)
+
+
 def solution(mesh):
+    plane = mesh.shape["tensor"] == 1 and mesh.shape["expert"] == 2 * GROUP
     return jax.shard_map(
-        body,
+        fast_body if plane else body,
         mesh=mesh,
         in_specs=(
             P(("groups", "expert"), None),

time: 582 us -> 168 us (0.29)
  the two profiles are of different devices: /device:TPU:11 before, /device:TPU:0 now
where the time goes in v1:
time: 168 us
  Pallas kernels  159 us (95%)
  other arithmetic  5.54 us (3%)
  local copies, waits for them, and re-layouts  2.06 us (1%)
    pallas_call x1, Pallas kernels, fast_body(): pl.pallas_call(functools.partial(expert_kernel, half_a), out_shape=jax.Sh...  104 us
    pallas_call x1, Pallas kernels, fast_body(): pl.pallas_call(gather_kernel, out_shape=[jax.ShapeDtypeStruct((count, wid...  54.9 us

profile of v1, /device:TPU:0, one launch (start us, length us, event | category | flops | bytes accessed | tf_op | source)
XLA Modules:
  0.0 167.5 jit_solution(7770219450325105848)
XLA Ops:
  0.7 0.7 fusion
  1.4 0.2 reduce_window_sum.11
  1.6 0.8 select_reduce_fusion
  2.4 0.7 multiply_add_fusion.1
  3.1 0.7 compare_convert_fusion.1.perm
  3.8 0.7 compare_convert_fusion.perm_t
  4.5 1.7 %pad_maximum_fusion.w_qkv = bf16[192,768]{1,0:T(8,128)(2,1)} fusion(bf16[192,256]{1,0:T(8,128)(2,1)} %param.18, bf16[192,256]{1,0:T(8,128)(2,1)} %param.17, bf16[192,256]{1,0:T(8,128)(2,1)} %param.16), kind=kLoop, calls=%fused_computation | loop fusion | flops 884736 | bytes 589824 | tf_op jit(solution)/shard_map/concatenate | solution.py:552
  6.2 54.9 %shard_map.118 = (bf16[128,3072]{1,0:T(8,128)(2,1)}, bf16[128,3072]{1,0:T(8,128)(2,1)}) custom-call(s32[1,1]{1,0:T(1,128)} %bitcast.5.lengths, bf16[128,3072]{1,0:T(8,128)(2,1)} %tokens.1, bf16[192,768]{1,0:T(8,128)(2,1)} %pad_maximum_fusion.w_qkv, bf16[192,256]{1,0:T(8,128)(2,1)} %w_out.1, f32[1,3072]{1,0:T(1,128)} %bitcast.6, f32[1,3072]{1,0:T(1,128)} %bitcast.7), custom_call_target="tpu_custom_call" | custom-call | tf_op jit(solution)/shard_map/pallas_call | solution.py:554
  61.1 104.3 %shard_map.119 = bf16[128,3072]{1,0:T(8,128)(2,1)} custom-call(bf16[128,3072]{1,0:T(8,128)(2,1)} %get-tuple-element.7.ein, bf16[128,3072]{1,0:T(8,128)(2,1)} %get-tuple-element.8.after, bf16[2,80,128]{2,1,0:T(8,128)(2,1)} %compare_convert_fusion.1.perm, bf16[2,128,80]{2,1,0:T(8,128)(2,1)} %compare_convert_fusion.perm_t, bf16[3072,1024]{1,0:T(8,128)(2,1)} %w_gate.1, ...), custom_call_target="tpu_custom_call" | custom-call | tf_op jit(solution)/shard_map/pallas_call | solution.py:587
  165.5 2.1 %copy.15 = bf16[128,3072]{1,0:T(8,128)(2,1)} copy(bf16[128,3072]{1,0:T(8,128)(2,1)} %shard_map.119) | data formatting | bytes 1572864
  (1 shorter events, 0.0 us)

commit v2 on v1

--- a/solution.py
+++ b/solution.py
@@ -166,37 +166,92 @@
 
 
 def gather_kernel(
-    lengths, tokens, w_qkv, w_out, gain, egain, after, ein, qkv_full, out_full, normed, ctx, send, recv, local
+    lengths,
+    tokens,
+    w_query,
+    w_key,
+    w_value,
+    w_out,
+    gain,
+    egain,
+    after,
+    ein,
+    qkv_full,
+    out_full,
+    normed,
+    ctx,
+    send,
+    recv,
+    local,
 ):
     me, core, x, z = place()
-    shard = w_out.shape[0]
+    plane = lax.axis_index("groups")
+    shard, heads = w_out.shape
+    third = shard // 3
     sib = me + 1 - 2 * core
     across = me + 2 - 4 * x
-    def rows(who):
-        return pl.ds(pl.multiple_of(who * shard, 64), shard)
-
     fulls = (qkv_full, out_full)
+
+    def rows(who, start, count):
+        return pl.ds(pl.multiple_of(who * shard + start, 64), count)
+
     copies = []
-    for g, own in enumerate((w_qkv, w_out)):
-        copy = pltpu.make_async_copy(own, fulls[g].at[rows(me)], local.at[g])
+    for k, own in enumerate((w_query, w_key, w_value)):
+        into = qkv_full.at[rows(me, 0, shard), pl.ds(k * heads, heads)]
+        copies.append(pltpu.make_async_copy(own, into, local.at[k]))
+    copies.append(pltpu.make_async_copy(w_out, out_full.at[rows(me, 0, shard)], local.at[3]))
+    for copy in copies:
         copy.start()
-        copies.append(copy)
-    wide = tokens[...].astype(F32)
-    mean_square = jnp.mean(wide * wide, axis=-1, keepdims=True)
-    normed[...] = (wide * lax.rsqrt(mean_square + 1e-05) * gain[...]).astype(BF16)
+    barrier = pltpu.get_barrier_semaphore()
+    other = {"groups": 1 - plane, "expert": me}
+    for target in (sib, across, (me + 4) % 16, (me + 12) % 16):
+        pl.semaphore_signal(
+            barrier, inc=1, device_id={"expert": target}, device_id_type=pl.DeviceIdType.MESH
+        )
+    pl.semaphore_signal(barrier, inc=1, device_id=other, device_id_type=pl.DeviceIdType.MESH)
     for copy in copies:
         copy.wait()
-    greet((sib, across, (me + 4) % 16, (me + 12) % 16))
-
-    targets = (me + 4, me - 4, across, sib)
+    pl.semaphore_wait(barrier, 5)
+
+    targets = (
+        {"expert": me + 4},
+        {"expert": me - 4},
+        {"expert": across},
+        {"expert": sib},
+        other,
+        {"expert": sib},
+    )
+
+    def block_of(g, direction, who):
+        start, count = third * plane, 2 * third
+        if direction == 4:
+            start, count = 2 * third * plane, third
+        elif direction == 5:
+            start, count = 2 * third * (1 - plane), third
+        return fulls[g].at[rows(who, start, count)]
 
     def move(g, direction, who):
-        block = fulls[g].at[rows(who)]
-        return remote(block, block, send.at[g, direction, who], recv.at[g, who], targets[direction])
+        block = block_of(g, direction, who)
+        return pltpu.make_async_remote_copy(
+            src_ref=block,
+            dst_ref=block,
+            send_sem=send.at[g, direction, who],
+            recv_sem=recv.at[g, direction // 4, who],
+            device_id=targets[direction],
+            device_id_type=pl.DeviceIdType.MESH,
+        )
 
     def arrived(g, who):
-        block = fulls[g].at[rows(who)]
-        remote(block, block, send.at[g, 0, who], recv.at[g, who], sib).wait_recv()
+        move(g, 3, who).wait_recv()
+
+    def arrived_third(g, who):
+        move(g, 5, who).wait_recv()
+
+    def start(copy):
+        copy.start()
+
+    def finish(copy):
+        copy.wait_send()
 
     def each_up(who, act, g):
         @pl.when(z < 3)
@@ -208,60 +263,91 @@
         def _():
             act(move(g, 1, who))
 
-    def start(copy):
-        copy.start()
-
-    def finish(copy):
-        copy.wait_send()
-
-    def column(g, act, wait):
+    def own(g, act):
         each_up(me, act, g)
         each_down(me, act, g)
         act(move(g, 2, me))
         act(move(g, 3, me))
-        for d in (1, 2, 3):
-
-            @pl.when(z >= d)
-            def _():
-                who = me - 4 * d
-                if wait:
-                    arrived(g, who)
-                each_up(who, act, g)
-                act(move(g, 2, who))
-                act(move(g, 3, who))
-
-            @pl.when(z + d <= 3)
-            def _():
-                who = me + 4 * d
-                if wait:
-                    arrived(g, who)
-                each_down(who, act, g)
-                act(move(g, 2, who))
-                act(move(g, 3, who))
-
+        act(move(g, 5, me))
+
+    def column(g, d, act, wait):
+        @pl.when(z >= d)
+        def _():
+            who = me - 4 * d
+            if wait:
+                arrived(g, who)
+            each_up(who, act, g)
+            for direction in (2, 4, 3):
+                act(move(g, direction, who))
+
+        @pl.when(z + d <= 3)
+        def _():
+            who = me + 4 * d
+            if wait:
+                arrived(g, who)
+            each_down(who, act, g)
+            for direction in (2, 4, 3):
+                act(move(g, direction, who))
+
+    def crossed(g, d, act, wait):
         def pass_on(who):
             if wait:
                 arrived(g, who)
+            act(move(g, 4, who))
             act(move(g, 3, who))
 
-        pass_on(across)
-        for d in (1, 2, 3):
-
-            @pl.when(z >= d)
-            def _():
-                pass_on(across - 4 * d)
-
-            @pl.when(z + d <= 3)
-            def _():
-                pass_on(across + 4 * d)
+        if d == 0:
+            pass_on(across)
+            return
+
+        @pl.when(z >= d)
+        def _():
+            pass_on(across - 4 * d)
+
+        @pl.when(z + d <= 3)
+        def _():
+            pass_on(across + 4 * d)
+
+    def thirds(g, d, act, wait):
+        def pass_on(who):
+            if wait:
+                arrived_third(g, who)
+            act(move(g, 5, who))
+
+        if d == 0:
+            pass_on(across)
+            return
+
+        @pl.when(z >= d)
+        def _():
+            pass_on(me - 4 * d)
+            pass_on(across - 4 * d)
+
+        @pl.when(z + d <= 3)
+        def _():
+            pass_on(me + 4 * d)
+            pass_on(across + 4 * d)
 
     def siblings(g):
         for zz in range(4):
             for xx in range(2):
                 arrived(g, (zz * 2 + xx) * 2 + 1 - core)
-
-    column(0, start, True)
-    column(1, start, True)
+                arrived_third(g, (zz * 2 + xx) * 2 + 1 - core)
+
+    own(0, start)
+    wide = tokens[...].astype(F32)
+    mean_square = jnp.mean(wide * wide, axis=-1, keepdims=True)
+    normed[...] = (wide * lax.rsqrt(mean_square + 1e-05) * gain[...]).astype(BF16)
+    for d in (1, 2, 3):
+        column(0, d, start, True)
+        crossed(0, d - 1, start, True)
+    own(1, start)
+    crossed(0, 3, start, True)
+    for d in (0, 1, 2, 3):
+        thirds(0, d, start, True)
+    for d in (1, 2, 3):
+        column(1, d, start, True)
+        crossed(1, d - 1, start, True)
     siblings(0)
 
     width = qkv_full.shape[1] // 3
@@ -283,6 +369,9 @@
         weights = jnp.exp(scores - peak)
         weights = (weights / jnp.sum(weights, axis=-1, keepdims=True)).astype(BF16)
         ctx[:, at : at + HEAD] = jnp.dot(weights, value, preferred_element_type=F32).astype(BF16)
+    crossed(1, 3, start, True)
+    for d in (0, 1, 2, 3):
+        thirds(1, d, start, True)
     siblings(1)
     attended = lax.dot_general(
         ctx[...], out_full[...], (((1,), (1,)), ((), ())), preferred_element_type=F32
@@ -291,16 +380,20 @@
     wide = after[...].astype(F32)
     mean_square = jnp.mean(wide * wide, axis=-1, keepdims=True)
     ein[...] = (wide * lax.rsqrt(mean_square + 1e-05) * egain[...]).astype(BF16)
-    column(0, finish, False)
-    column(1, finish, False)
+    for g in (0, 1):
+        own(g, finish)
+        for d in (0, 1, 2, 3):
+            if d:
+                column(g, d, finish, False)
+            crossed(g, d, finish, False)
+            thirds(g, d, finish, False)
 
 
 def expert_kernel(
     half_a,
     ein,
     after,
-    perm,
-    perm_t,
+    routed,
     w_gate,
     w_up,
     w_down,
@@ -341,8 +434,24 @@
         copy = pltpu.make_async_copy(src, dst, wsem.at[k])
         copy.start()
         loads.append(copy)
-    far_own[...] = jnp.dot(perm[1 - near], ein[...], preferred_element_type=F32).astype(BF16)
-    rows_in[0, 0] = jnp.dot(perm[near], ein[...], preferred_element_type=F32).astype(BF16)
+    count = ein.shape[0]
+    chosen = routed[...]
+    earlier = lax.broadcasted_iota(jnp.int32, (count, count), 0) <= lax.broadcasted_iota(
+        jnp.int32, (count, count), 1
+    )
+
+    def slot_matrix(expert):
+        named = jnp.broadcast_to(chosen == expert, (16, count))
+        number = jnp.dot(
+            named.astype(BF16), earlier.astype(BF16), preferred_element_type=F32
+        ).astype(jnp.int32)[0:1]
+        slot = lax.broadcasted_iota(jnp.int32, (cap, count), 0) + 1
+        return ((slot == number) & (chosen == expert)).astype(BF16)
+
+    far_pick = slot_matrix(1 - near)
+    near_pick = slot_matrix(near)
+    far_own[...] = jnp.dot(far_pick, ein[...], preferred_element_type=F32).astype(BF16)
+    rows_in[0, 0] = jnp.dot(near_pick, ein[...], preferred_element_type=F32).astype(BF16)
     greet((sib, across, along, mirror))
 
     started = []
@@ -511,8 +620,9 @@
     def finish(t):
         cols = pl.ds(pl.multiple_of(t * tile, tile), tile)
         returning(t).wait_recv()
-        moved = jnp.dot(perm_t[near], near_sum[t], preferred_element_type=F32)
-        moved = moved + jnp.dot(perm_t[1 - near], far_back[t], preferred_element_type=F32)
+        first = (((0,), (0,)), ((), ()))
+        moved = lax.dot_general(near_pick, near_sum[t], first, preferred_element_type=F32)
+        moved = moved + lax.dot_general(far_pick, far_back[t], first, preferred_element_type=F32)
         out[:, cols] = (after[:, cols].astype(F32) + moved).astype(BF16)
         returning(t).wait_send()
 
@@ -549,21 +659,20 @@
     vmem = pl.BlockSpec(memory_space=pltpu.VMEM)
     anywhere = pl.BlockSpec(memory_space=pl.ANY)
     heads = w_query.shape[1]
-    w_qkv = jnp.concatenate([w_query, w_key, w_value], axis=1)
     dma = pltpu.SemaphoreType.DMA
     after, ein = pl.pallas_call(
         gather_kernel,
         out_shape=[jax.ShapeDtypeStruct((count, width), BF16)] * 2,
-        in_specs=[vmem] * 6,
+        in_specs=[vmem] * 2 + [anywhere] * 4 + [vmem] * 2,
         out_specs=[vmem] * 2,
         scratch_shapes=[
             pltpu.VMEM((width, 3 * heads), BF16),
             pltpu.VMEM((width, heads), BF16),
             pltpu.VMEM((count, width), BF16),
             pltpu.VMEM((count, heads), BF16),
-            dma((2, 4, devices)),
-            dma((2, devices)),
-            dma((2,)),
+            dma((2, 6, devices)),
+            dma((2, 2, devices)),
+            dma((4,)),
         ],
         compiler_params=pltpu.CompilerParams(
             collective_id=0, has_side_effects=True, vmem_limit_bytes=VMEM_BYTES
@@ -571,23 +680,20 @@
     )(
         lengths.reshape(1, 1),
         tokens,
-        w_qkv,
+        w_query,
+        w_key,
+        w_value,
         w_out,
         attention_gain.reshape(1, width),
         expert_gain.reshape(1, width),
     )
-    slot_ids = slot_numbers(routed_expert, experts, capacity)
-    slots = jnp.arange(experts * capacity, dtype=jnp.int32)
-    perm = (slots[:, None] == slot_ids[None, :]).astype(BF16)
-    perm = perm.reshape(experts, capacity, count)
-    perm_t = jnp.swapaxes(perm, 1, 2)
     units = w_gate.shape[1]
     tile = width // TILES
     half_a = capacity * 3 // 5 // 16 * 16
     return pl.pallas_call(
         functools.partial(expert_kernel, half_a),
         out_shape=jax.ShapeDtypeStruct((count, width), BF16),
-        in_specs=[vmem] * 4 + [anywhere] * 3,
+        in_specs=[vmem] * 3 + [anywhere] * 3,
         out_specs=vmem,
         scratch_shapes=[
             pltpu.VMEM((width, units), BF16),
@@ -617,11 +723,12 @@
         compiler_params=pltpu.CompilerParams(
             collective_id=1, has_side_effects=True, vmem_limit_bytes=VMEM_BYTES
         ),
-    )(ein, after, perm, perm_t, w_gate, w_up, w_down)
+    )(ein, after, routed_expert.reshape(1, count), w_gate, w_up, w_down)
 
 
 def solution(mesh):
     plane = mesh.shape["tensor"] == 1 and mesh.shape["expert"] == 2 * GROUP
+    plane = plane and mesh.shape["groups"] == 2
     return jax.shard_map(
         fast_body if plane else body,
         mesh=mesh,

time: 168 us -> 157 us (0.935)
  other arithmetic: 5.54 us -> 0 us
  Pallas kernels: 159 us -> 154 us
    pallas_call x1, Pallas kernels: 54.9 us -> 46.3 us  [fast_body(): pl.pallas_call(gather_kernel, out_shape=[jax.ShapeDtypeStruct((count, wid...]
    pallas_call x1, Pallas kernels: 104 us -> 108 us  [fast_body(): pl.pallas_call(functools.partial(expert_kernel, half_a), out_shape=jax.Sh...]
    convert_element_type x3 -> x0, other arithmetic: 2.15 us -> none  [the longest x2 1.41 us: fast_body(): perm = (slots[:, None] == slot_ids[None, :]).astype(BF16)]
    concatenate x1 -> x0, other arithmetic: 1.72 us -> none  [fast_body(): w_qkv = jnp.concatenate([w_query, w_key, w_value], axis=1)]
where the time goes in v2:
time: 157 us
  Pallas kernels  154 us (98%)
  local copies, waits for them, and re-layouts  2.06 us (1%)
    pallas_call x1, Pallas kernels, fast_body(): pl.pallas_call(functools.partial(expert_kernel, half_a), out_shape=jax.Sh...  108 us
    pallas_call x1, Pallas kernels, fast_body(): pl.pallas_call(gather_kernel, out_shape=[jax.ShapeDtypeStruct((count, wid...  46.3 us

profile of v2, /device:TPU:0, one launch (start us, length us, event | category | flops | bytes accessed | tf_op | source)
XLA Modules:
  0.0 156.8 jit_solution(9642276896705879039)
XLA Ops:
  0.7 46.3 %shard_map.118 = (bf16[128,3072]{1,0:T(8,128)(2,1)}, bf16[128,3072]{1,0:T(8,128)(2,1)}) custom-call(s32[1,1]{1,0:T(1,128)} %bitcast.4.lengths, bf16[128,3072]{1,0:T(8,128)(2,1)} %tokens.1, bf16[192,256]{1,0:T(8,128)(2,1)} %w_query.1, bf16[192,256]{1,0:T(8,128)(2,1)} %w_key.1, bf16[192,256]{1,0:T(8,128)(2,1)} %w_value.1, bf16[192,256]{1,0:T(8,128)(2,1)} %w_out.1, ...), custom_call_target="tpu_custom_call" | custom-call | tf_op jit(solution)/shard_map/pallas_call | solution.py:663
  47.0 107.7 %shard_map.119 = bf16[128,3072]{1,0:T(8,128)(2,1)} custom-call(bf16[128,3072]{1,0:T(8,128)(2,1)} %get-tuple-element.7.ein, bf16[128,3072]{1,0:T(8,128)(2,1)} %get-tuple-element.8.after, s32[1,128]{1,0:T(1,128)} %bitcast.7, bf16[3072,1024]{1,0:T(8,128)(2,1)} %w_gate.1, bf16[3072,1024]{1,0:T(8,128)(2,1)} %w_up.1, bf16[1024,3072]{1,0:T(8,128)(2,1)} %w_down.1), custom_call_target="tpu_custom_call" | custom-call | tf_op jit(solution)/shard_map/pallas_call | solution.py:693
  154.7 2.1 %copy.15 = bf16[128,3072]{1,0:T(8,128)(2,1)} copy(bf16[128,3072]{1,0:T(8,128)(2,1)} %shard_map.119) | data formatting | bytes 1572864

commit v3 on v2

--- a/solution.py
+++ b/solution.py
@@ -454,63 +454,62 @@
     rows_in[0, 0] = jnp.dot(near_pick, ein[...], preferred_element_type=F32).astype(BF16)
     greet((sib, across, along, mirror))
 
-    started = []
-
-    def go(copy):
-        copy.start()
-        started.append(copy)
-        return copy
-
-    def gather_own(k):
-        own = rows_in.at[k, 0]
-        to_x = go(remote(own, rows_in.at[k, 1], gsend.at[k, 0], grecv.at[k, 0], across))
-        to_z = go(remote(own, rows_in.at[k, 2], gsend.at[k, 1], grecv.at[k, 1], along))
-        to_s = go(remote(own, rows_in.at[k, 4], gsend.at[k, 2], grecv.at[k, 2], sib))
-        return to_x, to_z, to_s
-
-    def gather_pass(k, first):
-        first[0].wait_recv()
-        from_x = rows_in.at[k, 1]
-        rest = cap - half_a
-        d_z = go(
-            remote(
-                from_x.at[pl.ds(half_a, rest)],
-                rows_in.at[k, 3, pl.ds(half_a, rest)],
-                gsend.at[k, 3],
-                grecv.at[k, 3],
-                along,
-            )
-        )
-        s1 = go(remote(from_x, rows_in.at[k, 5], gsend.at[k, 4], grecv.at[k, 4], sib))
-        first[1].wait_recv()
-        from_z = rows_in.at[k, 2]
-        d_x = go(
-            remote(
-                from_z.at[pl.ds(0, half_a)],
-                rows_in.at[k, 3, pl.ds(0, half_a)],
-                gsend.at[k, 5],
-                grecv.at[k, 5],
-                across,
-            )
-        )
-        s2 = go(remote(from_z, rows_in.at[k, 6], gsend.at[k, 6], grecv.at[k, 6], sib))
-        return d_z, d_x, s1, s2
-
-    def gather_last(k, second):
-        second[0].wait_recv()
-        second[1].wait_recv()
-        return go(
-            remote(rows_in.at[k, 3], rows_in.at[k, 7], gsend.at[k, 7], grecv.at[k, 7], sib)
-        )
-
-    def gather_done(first, second, third):
-        first[2].wait_recv()
-        second[2].wait_recv()
-        second[3].wait_recv()
-        third.wait_recv()
-
     fan = gate_v.shape[1] // TILES
     tile = width // TILES
+
+    def columns(t):
+        return pl.ds(pl.multiple_of(t * tile, tile), tile)
+
+    def gathering(kind, k, t):
+        cut = (half_a + 16, half_a)[k]
+        every, lower, upper = pl.ds(0, cap), pl.ds(0, cut), pl.ds(cut, cap - cut)
+        source, slot, rows, target = (
+            (0, 1, every, across),
+            (0, 2, every, along),
+            (0, 4, every, sib),
+            (1, 3, upper, along),
+            (1, 5, every, sib),
+            (2, 3, lower, across),
+            (2, 6, every, sib),
+            (3, 7, every, sib),
+        )[kind]
+        return remote(
+            rows_in.at[k, source, rows, columns(t)],
+            rows_in.at[k, slot, rows, columns(t)],
+            gsend.at[k, kind, t],
+            grecv.at[k, kind, t],
+            target,
+        )
+
+    def crossing(t):
+        return remote(
+            far_own.at[:, columns(t)],
+            rows_in.at[1, 0, :, columns(t)],
+            csem.at[0, t],
+            csem.at[1, t],
+            mirror,
+        )
+
+    def gather_own(k, t):
+        for kind in (0, 1, 2):
+            gathering(kind, k, t).start()
+
+    def gather_pass(k, t):
+        gathering(0, k, t).wait_recv()
+        gathering(3, k, t).start()
+        gathering(4, k, t).start()
+        gathering(1, k, t).wait_recv()
+        gathering(5, k, t).start()
+        gathering(6, k, t).start()
+
+    def gather_last(k, t):
+        gathering(3, k, t).wait_recv()
+        gathering(5, k, t).wait_recv()
+        gathering(7, k, t).start()
+
+    def gather_done(k, t):
+        for kind in (2, 4, 6, 7):
+            gathering(kind, k, t).wait_recv()
 
     def up_tile(k, t):
         cols = pl.ds(pl.multiple_of(t * fan, fan), fan)
@@ -520,7 +519,7 @@
         hidden[:, cols] = (jax.nn.silu(gate) * upward).astype(BF16)
 
     def down_tile(k, t):
-        cols = pl.ds(pl.multiple_of(t * tile, tile), tile)
+        cols = columns(t)
         total = jnp.dot(hidden[...], down_v[:, cols], preferred_element_type=F32)
         part[k * TILES + t] = total.astype(BF16).reshape(slots, cap, tile)
 
@@ -565,21 +564,32 @@
     def loop(body):
         lax.fori_loop(0, TILES, lambda t, c: (body(t), c)[1], 0)
 
-    near_first = gather_own(0)
-    crossing = go(remote(far_own, rows_in.at[1, 0], csem.at[0], csem.at[1], mirror))
-    near_second = gather_pass(0, near_first)
-    near_third = gather_last(0, near_second)
-    crossing.wait_recv()
-    far_first = gather_own(1)
-    gather_done(near_first, near_second, near_third)
+    def begin(t):
+        gather_own(0, t)
+        crossing(t).start()
+
+    def second(t):
+        gather_pass(0, t)
+        crossing(t).wait_recv()
+        gather_own(1, t)
+
+    loop(begin)
+    loop(second)
+    loop(functools.partial(gather_last, 0))
+    loop(functools.partial(gather_done, 0))
     for copy in loads:
         copy.wait()
-    loop(functools.partial(up_tile, 0))
-    far_second = gather_pass(1, far_first)
+
+    def near_up(t):
+        up_tile(0, t)
+        gather_pass(1, t)
+
+    loop(near_up)
 
     def near_down(t):
         down_tile(0, t)
         summing(0, t).start()
+        gather_last(1, t)
 
         @pl.when(t > 0)
         def _():
@@ -587,8 +597,7 @@
 
     loop(near_down)
     step_core(TILES - 1)
-    far_third = gather_last(1, far_second)
-    gather_done(far_first, far_second, far_third)
+    loop(functools.partial(gather_done, 1))
 
     def far_up(t):
         up_tile(1, t)
@@ -596,39 +605,50 @@
 
     loop(far_up)
 
-    def far_down(t):
+    def far_steps(t, c):
         i = TILES + t
-        down_tile(1, t)
-        summing(0, i).start()
-
-        @pl.when(t > 0)
+
+        @pl.when(t < TILES)
+        def _():
+            down_tile(1, t)
+            summing(0, i).start()
+            near_sum[t] = total_of(t)
+
+        @pl.when((t >= 1) & (t < TILES + 1))
         def _():
             step_core(i - 1)
 
-        near_sum[t] = total_of(t)
-
-    loop(far_down)
-    step_core(2 * TILES - 1)
-    loop(lambda t: step_diag(TILES + t))
-
-    def far_total(t):
-        far_sum[t] = total_of(TILES + t)
-        returning(t).start()
-
-    loop(far_total)
+        @pl.when((t >= 2) & (t < TILES + 2))
+        def _():
+            step_diag(i - 2)
+
+        @pl.when(t >= 3)
+        def _():
+            far_sum[t - 3] = total_of(i - 3)
+            returning(t - 3).start()
+
+        return c
+
+    lax.fori_loop(0, TILES + 3, far_steps, 0)
 
     def finish(t):
-        cols = pl.ds(pl.multiple_of(t * tile, tile), tile)
+        cols = columns(t)
         returning(t).wait_recv()
         first = (((0,), (0,)), ((), ()))
         moved = lax.dot_general(near_pick, near_sum[t], first, preferred_element_type=F32)
         moved = moved + lax.dot_general(far_pick, far_back[t], first, preferred_element_type=F32)
         out[:, cols] = (after[:, cols].astype(F32) + moved).astype(BF16)
+
+    loop(finish)
+
+    def drain_gather(t):
         returning(t).wait_send()
-
-    loop(finish)
-    for copy in started:
-        copy.wait_send()
+        crossing(t).wait_send()
+        for k in range(2):
+            for kind in range(8):
+                gathering(kind, k, t).wait_send()
+
+    loop(drain_gather)
 
     def drain(i, c):
         for kind in range(5):
@@ -712,9 +732,9 @@
             pltpu.VMEM((TILES, capacity, tile), BF16),
             pltpu.VMEM((TILES, capacity, tile), BF16),
             dma((3,)),
-            dma((2, 8)),
-            dma((2, 8)),
-            dma((2,)),
+            dma((2, 8, TILES)),
+            dma((2, 8, TILES)),
+            dma((2, TILES)),
             dma((5, 2 * TILES)),
             dma((5, 2 * TILES)),
             dma((TILES,)),

time: 157 us -> 151 us (0.962)
  Pallas kernels: 154 us -> 148 us
    pallas_call x1, Pallas kernels: 108 us -> 102 us  [fast_body(): pl.pallas_call(functools.partial(expert_kernel, half_a), out_shape=jax.Sh...]
where the time goes in v3:
time: 151 us
  Pallas kernels  148 us (98%)
  local copies, waits for them, and re-layouts  2.06 us (1%)
    pallas_call x1, Pallas kernels, fast_body(): pl.pallas_call(functools.partial(expert_kernel, half_a), out_shape=jax.Sh...  102 us
    pallas_call x1, Pallas kernels, fast_body(): pl.pallas_call(gather_kernel, out_shape=[jax.ShapeDtypeStruct((count, wid...  46.3 us

profile of v3, /device:TPU:0, one launch (start us, length us, event | category | flops | bytes accessed | tf_op | source)
XLA Modules:
  0.0 151.0 jit_solution(11525933227502226093)
XLA Ops:
  0.7 46.3 %shard_map.118 = (bf16[128,3072]{1,0:T(8,128)(2,1)}, bf16[128,3072]{1,0:T(8,128)(2,1)}) custom-call(s32[1,1]{1,0:T(1,128)} %bitcast.4.lengths, bf16[128,3072]{1,0:T(8,128)(2,1)} %tokens.1, bf16[192,256]{1,0:T(8,128)(2,1)} %w_query.1, bf16[192,256]{1,0:T(8,128)(2,1)} %w_key.1, bf16[192,256]{1,0:T(8,128)(2,1)} %w_value.1, bf16[192,256]{1,0:T(8,128)(2,1)} %w_out.1, ...), custom_call_target="tpu_custom_call" | custom-call | tf_op jit(solution)/shard_map/pallas_call | solution.py:683
  47.0 101.9 %shard_map.119 = bf16[128,3072]{1,0:T(8,128)(2,1)} custom-call(bf16[128,3072]{1,0:T(8,128)(2,1)} %get-tuple-element.7.ein, bf16[128,3072]{1,0:T(8,128)(2,1)} %get-tuple-element.8.after, s32[1,128]{1,0:T(1,128)} %bitcast.7, bf16[3072,1024]{1,0:T(8,128)(2,1)} %w_gate.1, bf16[3072,1024]{1,0:T(8,128)(2,1)} %w_up.1, bf16[1024,3072]{1,0:T(8,128)(2,1)} %w_down.1), custom_call_target="tpu_custom_call" | custom-call | tf_op jit(solution)/shard_map/pallas_call | solution.py:713
  148.9 2.1 %copy.15 = bf16[128,3072]{1,0:T(8,128)(2,1)} copy(bf16[128,3072]{1,0:T(8,128)(2,1)} %shard_map.119) | data formatting | bytes 1572864

commit v4 on v3

--- a/solution.py
+++ b/solution.py
@@ -403,6 +403,8 @@
     down_v,
     rows_in,
     far_own,
+    gate_sum,
+    up_sum,
     hidden,
     part,
     from_sib,
@@ -427,7 +429,7 @@
     sib = me + 1 - 2 * core
     across = me + 2 - 4 * x
     along = me + 4 - 8 * (z % 2)
-    mirror = me + 8 - 16 * near
+    mirror = me + 12 - 8 * z
     slots, cap, width = rows_in.shape[1], rows_in.shape[2], rows_in.shape[3]
     loads = []
     for k, (src, dst) in enumerate(((w_gate, gate_v), (w_up, up_v), (w_down, down_v))):
@@ -511,12 +513,31 @@
         for kind in (2, 4, 6, 7):
             gathering(kind, k, t).wait_recv()
 
-    def up_tile(k, t):
+    def up_part(k, t):
+        given = rows_in[k, :, :, columns(t)].reshape(slots * cap, tile)
+
+        def block(j, c):
+            cols = pl.ds(pl.multiple_of(j * fan, fan), fan)
+            gate = jnp.dot(given, gate_v[columns(t), cols], preferred_element_type=F32)
+            upward = jnp.dot(given, up_v[columns(t), cols], preferred_element_type=F32)
+
+            @pl.when(t == 0)
+            def _():
+                gate_sum[:, cols] = gate
+                up_sum[:, cols] = upward
+
+            @pl.when(t > 0)
+            def _():
+                gate_sum[:, cols] += gate
+                up_sum[:, cols] += upward
+
+            return c
+
+        lax.fori_loop(0, TILES, block, 0)
+
+    def activate(t):
         cols = pl.ds(pl.multiple_of(t * fan, fan), fan)
-        given = rows_in[k].reshape(slots * cap, width)
-        gate = jnp.dot(given, gate_v[:, cols], preferred_element_type=F32)
-        upward = jnp.dot(given, up_v[:, cols], preferred_element_type=F32)
-        hidden[:, cols] = (jax.nn.silu(gate) * upward).astype(BF16)
+        hidden[:, cols] = (jax.nn.silu(gate_sum[:, cols]) * up_sum[:, cols]).astype(BF16)
 
     def down_tile(k, t):
         cols = columns(t)
@@ -576,15 +597,16 @@
     loop(begin)
     loop(second)
     loop(functools.partial(gather_last, 0))
-    loop(functools.partial(gather_done, 0))
     for copy in loads:
         copy.wait()
 
     def near_up(t):
-        up_tile(0, t)
+        gather_done(0, t)
+        up_part(0, t)
         gather_pass(1, t)
 
     loop(near_up)
+    loop(activate)
 
     def near_down(t):
         down_tile(0, t)
@@ -597,13 +619,13 @@
 
     loop(near_down)
     step_core(TILES - 1)
-    loop(functools.partial(gather_done, 1))
-
     def far_up(t):
-        up_tile(1, t)
+        gather_done(1, t)
+        up_part(1, t)
         step_diag(t)
 
     loop(far_up)
+    loop(activate)
 
     def far_steps(t, c):
         i = TILES + t
@@ -721,6 +743,8 @@
             pltpu.VMEM((units, width), BF16),
             pltpu.VMEM((2, 8, capacity, width), BF16),
             pltpu.VMEM((capacity, width), BF16),
+            pltpu.VMEM((8 * capacity, units), F32),
+            pltpu.VMEM((8 * capacity, units), F32),
             pltpu.VMEM((8 * capacity, units), BF16),
             pltpu.VMEM((2 * TILES, 8, capacity, tile), BF16),
             pltpu.VMEM((2 * TILES, 4, capacity, tile), BF16),

time: 151 us -> 161 us (1.066)
  Pallas kernels: 148 us -> 158 us
    pallas_call x1, Pallas kernels: 102 us -> 112 us  [fast_body(): pl.pallas_call(functools.partial(expert_kernel, half_a), out_shape=jax.Sh...]
where the time goes in v4:
time: 161 us
  Pallas kernels  158 us (98%)
  local copies, waits for them, and re-layouts  2.06 us (1%)
    pallas_call x1, Pallas kernels, fast_body(): pl.pallas_call(functools.partial(expert_kernel, half_a), out_shape=jax.Sh...  112 us
    pallas_call x1, Pallas kernels, fast_body(): pl.pallas_call(gather_kernel, out_shape=[jax.ShapeDtypeStruct((count, wid...  46.3 us

profile of v4, /device:TPU:0, one launch (start us, length us, event | category | flops | bytes accessed | tf_op | source)
XLA Modules:
  0.0 161.2 jit_solution(845413177032039663)
XLA Ops:
  0.7 46.3 %shard_map.118 = (bf16[128,3072]{1,0:T(8,128)(2,1)}, bf16[128,3072]{1,0:T(8,128)(2,1)}) custom-call(s32[1,1]{1,0:T(1,128)} %bitcast.4.lengths, bf16[128,3072]{1,0:T(8,128)(2,1)} %tokens.1, bf16[192,256]{1,0:T(8,128)(2,1)} %w_query.1, bf16[192,256]{1,0:T(8,128)(2,1)} %w_key.1, bf16[192,256]{1,0:T(8,128)(2,1)} %w_value.1, bf16[192,256]{1,0:T(8,128)(2,1)} %w_out.1, ...), custom_call_target="tpu_custom_call" | custom-call | tf_op jit(solution)/shard_map/pallas_call | solution.py:705
  47.0 112.1 %shard_map.119 = bf16[128,3072]{1,0:T(8,128)(2,1)} custom-call(bf16[128,3072]{1,0:T(8,128)(2,1)} %get-tuple-element.7.ein, bf16[128,3072]{1,0:T(8,128)(2,1)} %get-tuple-element.8.after, s32[1,128]{1,0:T(1,128)} %bitcast.7, bf16[3072,1024]{1,0:T(8,128)(2,1)} %w_gate.1, bf16[3072,1024]{1,0:T(8,128)(2,1)} %w_up.1, bf16[1024,3072]{1,0:T(8,128)(2,1)} %w_down.1), custom_call_target="tpu_custom_call" | custom-call | tf_op jit(solution)/shard_map/pallas_call | solution.py:735
  159.1 2.1 %copy.15 = bf16[128,3072]{1,0:T(8,128)(2,1)} copy(bf16[128,3072]{1,0:T(8,128)(2,1)} %shard_map.119) | data formatting | bytes 1572864
